TPU v7x, 32 devices: a whole 2x2x4 slice. The times are simulated.
32 devices in a mesh: angle: 4 (over y, x), gz: 8 (over z, core).
Axes of the slice: x: 2, y: 2, z: 4, core: 2. Of those that a mesh axis runs over, the one named last changes fastest.
Arguments:
- volume: bfloat16 [8, 512, 512], P('gz'), may hold values from -0.3984375 to 0.3984375
- probe: float32 [8, 2, 128, 128], replicated, may hold values from -0.046875 to 0.046875
- measured: float32 [4, 8, 128, 128], P('angle', 'gz'), may hold values from 2 to 40
- angle_index: int32 [4], P('angle'), may hold values from 0 to 3, each once
- row_offset: int32 [4, 8], P('angle', 'gz'), may hold values from -64 to -56, as said below
- col_offset: int32 [4, 8], P('angle', 'gz'), may hold values from 0 to 384, as said below
Outputs:
- volume_update: float32 [8, 512, 512], P('gz', 'angle')
- probe_update: float32 [8, 2, 128, 128], replicated
Inputs may be any that keep to these rules, and one draw needn't show every extreme that they name: `row_offset`: windows may reach 64 rows past either end of the projection; both ends are used. `col_offset`: both ends are used. `angle_index`: each angle number once.
All inputs are finite; a program needn't handle non-finite values.
Results may differ from a plain program's by a relative error of at most 0.0005.
Values sent between devices are 32-bit elements; how exact they have to be, the bound alone decides.
A program may use at most 64 MiB of HBM per device.

v0:
```python
import functools
import math

import jax
import jax.numpy as jnp
import numpy as np
from jax import lax
from jax.experimental import pallas as pl
from jax.experimental.pallas import tpu as pltpu
from jax.sharding import PartitionSpec as P

MESH = pl.DeviceIdType.MESH
F32 = jnp.float32
BF16 = jnp.bfloat16
VM = pl.BlockSpec(memory_space=pltpu.VMEM)
SM = pl.BlockSpec(memory_space=pltpu.SMEM)


def split_table(table):
    table = np.asarray(table, np.float32)
    high = table.astype(jnp.bfloat16)
    low = (table - high.astype(np.float32)).astype(jnp.bfloat16)
    return np.stack([high, low])


def split(value):
    high = value.astype(BF16)
    return high, (value - high.astype(F32)).astype(BF16)


def dot(a, b):
    return jnp.dot(a, b, preferred_element_type=F32)


def dot3(a, b):
    return dot(a[0], b[0]) + (dot(a[0], b[1]) + dot(a[1], b[0]))


def packed_forward(n):
    k = np.arange(n // 2)[:, None]
    x = np.arange(n)[None, :]
    turns = 2.0 * np.pi * (k * x % n) / n
    imag = -np.sin(turns)
    imag[0] = np.where(x[0] % 2 == 0, 1.0, -1.0)
    return np.concatenate([np.cos(turns), imag], axis=0)


def wave_tables(n):
    k = np.arange(n // 2)[:, None]
    y = np.arange(n)[None, :]
    turns = 2.0 * np.pi * (k * y % n) / n
    sine = np.sin(turns)
    sine[0] = np.where(y[0] % 2 == 0, 1.0, -1.0)
    return np.stack([np.cos(turns), sine]).astype(np.float32)


def angle_tables(nx, ny, count):
    rot, mix = [], []
    cells_y = np.arange(ny)[None, :] - ny / 2
    cells_x = np.arange(nx)[None, :] - nx / 2
    weight = np.full(nx // 2, 2.0 / nx)
    weight[0] = 1.0 / nx
    for number in range(count):
        theta = math.pi * (number + 0.5) / count - math.pi / 2
        shear_x = -math.tan(theta / 2)
        shear_y = math.sin(theta)
        kx = np.arange(nx // 2)[:, None]
        one = -2.0 * np.pi * kx * shear_x * cells_y / nx
        nyquist_one = 2.0 * np.pi * (nx // 2) * shear_x * cells_y[0] / nx
        sine = np.sin(one)
        sine[0] = np.cos(nyquist_one)
        rot.append(np.stack([np.cos(one), sine]))
        ky = np.arange(ny // 2)[:, None]
        two = -2.0 * np.pi * ky * shear_y * cells_x / ny
        nyquist_two = 2.0 * np.pi * (ny // 2) * shear_y * cells_x[0] / ny
        upper, lower = np.cos(two), np.sin(two)
        lower[0] = np.cos(nyquist_two)
        spectrum = np.fft.rfft(np.concatenate([upper, lower], axis=0), axis=1)
        real = spectrum.real[:, : nx // 2] * weight
        imag = spectrum.imag[:, : nx // 2] * weight
        imag[:, 0] = spectrum.real[:, nx // 2] / nx
        mix.append(np.concatenate([real, imag], axis=1))
    return np.stack(rot).astype(np.float32), np.stack(mix)


def first_row(shape):
    return lax.broadcasted_iota(jnp.int32, shape, 0) == 0


def half_weights(n):
    return jnp.where(first_row((n // 2, 1)), 1.0 / n, 2.0 / n).astype(F32)


def forward_kernel(number, volume, fx, rot, mix, wave, out):
    n = volume.shape[1]
    half = n // 2
    field = volume[0]
    spec = dot(fx[0], field) + dot(fx[1], field)
    real, imag = spec[:half], spec[half:]
    top = first_row((half, 1))
    cosine, raw = rot[0, 0], rot[0, 1]
    sine = jnp.where(top, 0.0, raw)
    turned = jnp.concatenate(
        [real * cosine - imag * sine, real * sine + imag * jnp.where(top, raw, cosine)], axis=0
    )
    beam = dot3((mix[0, 0], mix[1, 0]), split(turned))
    upper, lower = beam[:half], beam[half:]
    cosine, raw = wave[0], wave[1]
    sine = jnp.where(top, 0.0, raw)
    weight = half_weights(wave.shape[2])
    sum_real = weight * jnp.sum(upper * cosine + lower * sine, axis=1, keepdims=True)
    sum_imag = weight * jnp.sum(
        lower * jnp.where(top, raw, cosine) - upper * sine, axis=1, keepdims=True
    )
    out[...] = jnp.sum(
        sum_real * cosine - sum_imag * jnp.where(top, -raw, raw), axis=0, keepdims=True
    )


def exact_dot(a, b):
    return jnp.dot(a, b, precision=lax.Precision.HIGHEST, preferred_element_type=F32)


def window_kernel(
    modes, row_off, col_off, number, row, probe, measured, turn,
    grad_rows, probe_grad,
    gathered, sent, received, angle_sent, angle_rows, mat, wide,
    gs, gr, rs, rr, as_, ar,
):
    depth, angles = gathered.shape[0], angle_rows.shape[0]
    width = row.shape[1]
    window = probe.shape[-1]
    half = window // 2
    g, a = lax.axis_index("gz"), lax.axis_index("angle")

    barrier = pltpu.get_barrier_semaphore()
    for d in range(1, depth):
        pl.semaphore_signal(barrier, inc=1, device_id=(a, lax.rem(g + d, depth)), device_id_type=MESH)
    for d in range(1, angles):
        pl.semaphore_signal(barrier, inc=1, device_id=(lax.rem(a + d, angles), g), device_id_type=MESH)
    pl.semaphore_wait(barrier, depth + angles - 2)

    def push(src, dst, send, recv, device):
        return pltpu.make_async_remote_copy(
            src_ref=src, dst_ref=dst, send_sem=send, recv_sem=recv, device_id=device, device_id_type=MESH
        )

    copies = []
    for d in range(1, depth):
        copies.append(push(row, gathered.at[g], gs.at[d], gr.at[d], (a, lax.rem(g + d, depth))))
        copies[-1].start()
    gathered[g] = row[...]
    for copy in copies:
        copy.wait()

    rows = jnp.concatenate([gathered[z] for z in range(depth)], axis=0)
    row0, col0 = row_off[0, 0], col_off[0, 0]
    iota = lax.broadcasted_iota
    pick = (iota(jnp.int32, (width, window), 0) == iota(jnp.int32, (width, window), 1) + col0).astype(F32)
    pick_t = (iota(jnp.int32, (window, width), 1) == iota(jnp.int32, (window, width), 0) + col0).astype(F32)
    shape = (2 * depth, depth)
    place = (
        iota(jnp.int32, shape, 0) + (half - depth) == iota(jnp.int32, shape, 1) - row0
    ).astype(F32)
    place_t = (
        iota(jnp.int32, shape[::-1], 1) + (half - depth) == iota(jnp.int32, shape[::-1], 0) - row0
    ).astype(F32)
    patch = exact_dot(place, exact_dot(rows, pick))
    obj_real, obj_imag = jnp.cos(patch), jnp.sin(patch)
    low, high = half - depth, half + depth

    for m in range(modes):
        lanes = slice(m * window, (m + 1) * window)
        mat[0:window, lanes] = probe[m, 0]
        mat[window:, lanes] = probe[m, 1]
        mid_real, mid_imag = probe[m, 0, low:high], probe[m, 1, low:high]
        mat[low:high, lanes] = mid_real * obj_real - mid_imag * obj_imag
        mat[window + low : window + high, lanes] = mid_real * obj_imag + mid_imag * obj_real
    left, left_t = (turn[0, 0], turn[0, 1]), (turn[1, 0], turn[1, 1])
    mat[...] = dot3(left, split(mat[...]))
    for m in range(modes):
        lanes = slice(m * window, (m + 1) * window)
        wide[lanes, 0:window] = mat[0:window, lanes]
        wide[lanes, window:] = mat[window:, lanes]
    wide[...] = dot3(split(wide[...]), left_t)
    intensity = jnp.zeros((window, window), F32)
    for m in range(modes):
        lanes = slice(m * window, (m + 1) * window)
        far_real, far_imag = wide[lanes, 0:window], wide[lanes, window:]
        intensity += far_real * far_real + far_imag * far_imag
    factor = (1.0 - jnp.sqrt(measured[0, 0] + 1.0) / jnp.sqrt(intensity + 1.0)) / window
    for m in range(modes):
        lanes = slice(m * window, (m + 1) * window)
        wide[lanes, 0:window] = wide[lanes, 0:window] * factor
        wide[lanes, window:] = wide[lanes, window:] * factor
    wide[...] = dot3(split(wide[...]), left)
    for m in range(modes):
        lanes = slice(m * window, (m + 1) * window)
        mat[0:window, lanes] = wide[lanes, 0:window]
        mat[window:, lanes] = wide[lanes, window:]
    mat[...] = dot3(left_t, split(mat[...]))

    grad_real = jnp.zeros((2 * depth, window), F32)
    grad_imag = jnp.zeros((2 * depth, window), F32)
    for m in range(modes):
        lanes = slice(m * window, (m + 1) * window)
        back_real, back_imag = mat[low:high, lanes], mat[window + low : window + high, lanes]
        mid_real, mid_imag = probe[m, 0, low:high], probe[m, 1, low:high]
        grad_real += mid_real * back_real + mid_imag * back_imag
        grad_imag += mid_real * back_imag - mid_imag * back_real
    patch_grad = grad_imag * obj_real - grad_real * obj_imag
    full = exact_dot(exact_dot(place_t, patch_grad), pick_t)
    for z in range(depth):
        sent[z] = full[z : z + 1]

    copies = []
    for d in range(1, depth):
        peer = lax.rem(g + d, depth)
        copies.append(push(sent.at[peer], received.at[g], rs.at[d], rr.at[d], (a, peer)))
        copies[-1].start()
    received[g] = sent[g]

    for m in range(modes):
        lanes = slice(m * window, (m + 1) * window)
        probe_grad[m, 0] = mat[0:window, lanes] * 0.0625
        probe_grad[m, 1] = mat[window:, lanes] * 0.0625
        back_real, back_imag = mat[low:high, lanes], mat[window + low : window + high, lanes]
        probe_grad[m, 0, low:high] = (obj_real * back_real + obj_imag * back_imag) * 0.0625
        probe_grad[m, 1, low:high] = (obj_real * back_imag - obj_imag * back_real) * 0.0625

    for copy in copies:
        copy.wait()
    total = received[0]
    for z in range(1, depth):
        total = total + received[z]
    angle_sent[:, 0:width] = total
    angle_sent[:, width:] = jnp.zeros((1, 128), F32) + number[0].astype(F32)
    copies = []
    for d in range(1, angles):
        copies.append(push(angle_sent, angle_rows.at[a], as_.at[d], ar.at[d], (lax.rem(a + d, angles), g)))
        copies[-1].start()
    angle_rows[a] = angle_sent[...]
    for copy in copies:
        copy.wait()
    grad_rows[...] = angle_rows[...]


def back_kernel(block, grad_rows, rot, mix_t, wave, fx_t, out, acc):
    step, angles = pl.program_id(0), pl.num_programs(0)
    half, width = wave.shape[1], wave.shape[2]
    row = jnp.zeros((1, width), F32)
    for a in range(grad_rows.shape[0]):
        mine = grad_rows[a, :, width : width + 1] == step.astype(F32)
        row = row + jnp.where(mine, grad_rows[a, :, 0:width], 0.0)
    top = first_row((half, 1))
    cosine, raw = wave[0], wave[1]
    sine = jnp.where(top, 0.0, raw)
    weight = half_weights(width)
    in_real = weight * jnp.sum(row * cosine, axis=1, keepdims=True)
    in_imag = -weight * jnp.sum(row * jnp.where(top, -raw, raw), axis=1, keepdims=True)
    beam = jnp.concatenate(
        [in_real * cosine - in_imag * sine, in_real * sine + in_imag * jnp.where(top, raw, cosine)], axis=0
    )
    turned = dot3((mix_t[0, 0], mix_t[1, 0]), split(beam))
    kx = turned.shape[0] // 2
    real, imag = turned[:kx], turned[kx:]
    top = first_row((kx, 1))
    cosine, raw = rot[0, 0], rot[0, 1]
    sine = jnp.where(top, 0.0, raw)
    back = jnp.concatenate(
        [real * cosine + imag * sine, imag * jnp.where(top, raw, cosine) - real * sine], axis=0
    )

    @pl.when(step == 0)
    def _():
        acc[...] = back

    @pl.when(step > 0)
    def _():
        acc[...] += back

    @pl.when(step == angles - 1)
    def _():
        out[0] = 4.0 * dot3((fx_t[0], fx_t[1]), split(acc[...]))


def local(volume, probe, measured, angle_index, row_offset, col_offset):
    _, nx, ny = volume.shape
    modes, _, window, _ = probe.shape
    depth, angles = lax.axis_size("gz"), lax.axis_size("angle")
    rot, mix = angle_tables(nx, ny, angles)
    mix_pair = split_table(mix)
    mix_t_pair = split_table(np.swapaxes(mix, 1, 2))
    fx = packed_forward(nx)
    fx_pair, fx_t_pair = split_table(fx), split_table(fx.T)
    wave = wave_tables(ny)
    turns = 2.0 * np.pi * (np.arange(window)[:, None] * np.arange(window)[None, :] % window) / window
    cosine, sine = np.cos(turns), np.sin(turns)
    left = np.block([[cosine, sine], [-sine, cosine]])
    turn = np.stack([split_table(left), split_table(left.T)])
    big = 48 * 1024 * 1024

    row = pl.pallas_call(
        forward_kernel,
        grid_spec=pltpu.PrefetchScalarGridSpec(
            num_scalar_prefetch=1,
            grid=(1,),
            in_specs=[
                pl.BlockSpec((1, nx, ny), lambda i, s: (0, 0, 0)),
                pl.BlockSpec((2, nx, nx), lambda i, s: (0, 0, 0)),
                pl.BlockSpec((1, 2, nx // 2, ny), lambda i, s: (s[0], 0, 0, 0)),
                pl.BlockSpec((2, 1, ny, nx), lambda i, s: (0, s[0], 0, 0)),
                pl.BlockSpec((2, ny // 2, ny), lambda i, s: (0, 0, 0)),
            ],
            out_specs=pl.BlockSpec((1, ny), lambda i, s: (0, 0)),
        ),
        out_shape=jax.ShapeDtypeStruct((1, ny), F32),
        compiler_params=pltpu.CompilerParams(vmem_limit_bytes=big),
        name="forward",
    )(angle_index, volume, fx_pair, rot, mix_pair, wave)

    dma = pltpu.SemaphoreType.DMA
    grad_rows, probe_grad = pl.pallas_call(
        functools.partial(window_kernel, modes),
        out_shape=(
            jax.ShapeDtypeStruct((angles, 1, ny + 128), F32),
            jax.ShapeDtypeStruct(probe.shape, F32),
        ),
        in_specs=[SM, SM, SM, VM, VM, VM, VM],
        out_specs=(VM, VM),
        scratch_shapes=[
            pltpu.VMEM((depth, 1, ny), F32),
            pltpu.VMEM((depth, 1, ny), F32),
            pltpu.VMEM((depth, 1, ny), F32),
            pltpu.VMEM((1, ny + 128), F32),
            pltpu.VMEM((angles, 1, ny + 128), F32),
            pltpu.VMEM((2 * window, modes * window), F32),
            pltpu.VMEM((modes * window, 2 * window), F32),
            dma((depth,)), dma((depth,)), dma((depth,)), dma((depth,)), dma((angles,)), dma((angles,)),
        ],
        compiler_params=pltpu.CompilerParams(
            collective_id=0, has_side_effects=True, vmem_limit_bytes=big
        ),
        name="window",
    )(row_offset, col_offset, angle_index, row, probe, measured, turn)

    probe_total = lax.psum(probe_grad, ("angle", "gz"))

    block = jnp.reshape(lax.axis_index("angle"), (1,)).astype(jnp.int32)
    block_rows = nx // angles
    out = pl.pallas_call(
        back_kernel,
        grid_spec=pltpu.PrefetchScalarGridSpec(
            num_scalar_prefetch=1,
            grid=(angles,),
            in_specs=[
                pl.BlockSpec((angles, 1, ny + 128), lambda i, s: (0, 0, 0)),
                pl.BlockSpec((1, 2, nx // 2, ny), lambda i, s: (i, 0, 0, 0)),
                pl.BlockSpec((2, 1, nx, ny), lambda i, s: (0, i, 0, 0)),
                pl.BlockSpec((2, ny // 2, ny), lambda i, s: (0, 0, 0)),
                pl.BlockSpec((2, block_rows, nx), lambda i, s: (0, s[0], 0)),
            ],
            out_specs=pl.BlockSpec((1, block_rows, ny), lambda i, s: (0, 0, 0)),
            scratch_shapes=[pltpu.VMEM((nx, ny), F32)],
        ),
        out_shape=jax.ShapeDtypeStruct((1, block_rows, ny), F32),
        compiler_params=pltpu.CompilerParams(vmem_limit_bytes=big),
        cost_estimate=pl.CostEstimate(flops=4_000_000_000, bytes_accessed=9_000_000, transcendentals=0),
        name="back",
    )(block, grad_rows, rot, mix_t_pair, wave, fx_t_pair)
    return (out, probe_total)


def solution(mesh):
    return jax.shard_map(
        local,
        mesh=mesh,
        in_specs=(
            P("gz", None, None),
            P(),
            P("angle", "gz", None, None),
            P("angle"),
            P("angle", "gz"),
            P("angle", "gz"),
        ),
        out_specs=(P("gz", "angle", None), P()),
        check_vma=False,
    )
```

profile of v0, /device:TPU:0, one launch (start us, length us, event | category | flops | bytes accessed | tf_op | source)
XLA Modules:
  0.0 174.9 jit_solution(2314795098625644440)
XLA Ops:
  7.2 0.0 all-reduce.2.cloned.1.call-start
  9.1 0.0 copy-start
  9.2 1.2 copy-done
  10.4 0.0 copy-start.2
  10.4 1.2 copy-done.2
  11.6 0.0 copy-start.4
  11.6 1.0 copy-done.4
  12.6 0.0 copy-start.3
  12.6 0.0 copy-start.5
  12.6 0.0 copy-start.6
  12.7 0.0 copy-start.1
  12.7 0.0 copy-start.7
  12.7 3.6 %forward.1.row = f32[1,512]{1,0:T(1,128)S(1)} custom-call(s32[1]{0:T(128)S(6)} %copy.17.number, bf16[1,512,512]{2,1,0:T(8,128)(2,1)S(1)} %copy-done.4, bf16[2,512,512]{2,1,0:T(8,128)(2,1)S(1)} %copy-done.2, f32[4,2,256,512]{3,2,1,0:T(8,128)} %constant.20.clone.rot, bf16[2,4,512,512]{3,2,1,0:T(8,128)(2,1)} %constant.21.clone.mix, f32[2,256,512]{2,1,0:T(8,128)S(1)} %copy-done), custom_call_target="tpu_custom_call" | custom-call | tf_op jit(solution)/shard_map/forward/pallas_call | solution.py:303
  16.3 0.0 copy-done.3
  16.3 0.0 copy-done.5
  16.3 0.0 copy-done.6
  16.3 21.2 %window.1 = (f32[4,1,640]{2,1,0:T(1,128)S(1)}, f32[8,2,128,128]{3,2,1,0:T(8,128)}) custom-call(s32[1,1]{1,0:T(1,128)S(6)} %copy.18.row_off, s32[1,1]{1,0:T(1,128)S(6)} %copy.19.col_off, s32[1]{0:T(128)S(6)} %copy.17.number, f32[1,512]{1,0:T(1,128)S(1)} %forward.1.row, f32[8,2,128,128]{3,2,1,0:T(8,128)S(1)} %copy-done.3, f32[1,1,128,128]{3,2,1,0:T(8,128)S(1)} %copy-done.6, ...), custom_call_target="tpu_custom_call" | custom-call | tf_op jit(solution)/shard_map/window/pallas_call | solution.py:323
  37.5 0.0 all-reduce.2.cloned.1.call-update
  37.6 0.0 copy-done.1
  37.6 0.0 copy-done.7
  37.6 8.6 %back.1 = f32[1,128,512]{2,1,0:T(8,128)} custom-call(s32[1]{0:T(128)} %bitcast.block, f32[4,1,640]{2,1,0:T(1,128)S(1)} %get-tuple-element.4.grad_rows, f32[4,2,256,512]{3,2,1,0:T(8,128)} %constant.20.clone.rot, bf16[2,4,512,512]{3,2,1,0:T(8,128)(2,1)} %constant.24.clone.mix_t, f32[2,256,512]{2,1,0:T(8,128)S(1)} %copy-done.1, bf16[2,512,512]{2,1,0:T(8,128)(2,1)S(1)} %copy-done.7), custom_call_target="tpu_custom_call" | custom-call | flops 4000000000 | bytes 9000000 | tf_op jit(solution)/shard_map/back/pallas_call | solution.py:351
  46.2 119.6 %all-reduce.2.cloned.1.call-done = f32[8,2,128,128]{3,2,1,0:T(8,128)} async-done(((f32[8,2,128,128]{3,2,1,0:T(8,128)}), f32[8,2,128,128]{3,2,1,0:T(8,128)}) %all-reduce.2.cloned.1.call-update) | async-done | bytes 1048592 | tf_op jit(solution)/shard_map/psum | solution.py:347
  165.7 2.3 %copy.20 = f32[8,2,128,128]{3,2,1,0:T(8,128)} copy(f32[8,2,128,128]{3,2,1,0:T(8,128)} %all-reduce.2.cloned.1.call-done) | data formatting | bytes 2097152
Async XLA Ops:
  7.2 158.6 %all-reduce.2.cloned.1.call-start = ((), (), s32[]{:S(2)}) async-start(), calls=%async_computation | async-start | bytes 2097152 | tf_op jit(solution)/shard_map/psum | solution.py:347
  9.1 1.2 copy-start
  10.4 1.2 copy-start.2
  11.6 1.0 copy-start.4
  12.6 3.7 %copy-start.3 = (f32[8,2,128,128]{3,2,1,0:T(8,128)S(1)}, f32[8,2,128,128]{3,2,1,0:T(8,128)}, u32[]{:S(2)}) copy-start(f32[8,2,128,128]{3,2,1,0:T(8,128)} %probe.1) | copy-start | bytes 3145732
  12.6 3.7 %copy-start.5 = (bf16[2,2,256,256]{3,2,1,0:T(8,128)(2,1)S(1)}, bf16[2,2,256,256]{3,2,1,0:T(8,128)(2,1)}, u32[]{:S(2)}) copy-start(bf16[2,2,256,256]{3,2,1,0:T(8,128)(2,1)} %constant.23.clone.turn) | copy-start | bytes 1572868
  12.6 3.7 %copy-start.6 = (f32[1,1,128,128]{3,2,1,0:T(8,128)S(1)}, f32[1,1,128,128]{3,2,1,0:T(8,128)}, u32[]{:S(2)}) copy-start(f32[1,1,128,128]{3,2,1,0:T(8,128)} %measured.1) | copy-start | bytes 196612
  12.7 24.9 %copy-start.1 = (f32[2,256,512]{2,1,0:T(8,128)S(1)}, f32[2,256,512]{2,1,0:T(8,128)}, u32[]{:S(2)}) copy-start(f32[2,256,512]{2,1,0:T(8,128)} %constant.22.clone.wave) | copy-start | bytes 3145732
  12.7 24.9 %copy-start.7 = (bf16[2,512,512]{2,1,0:T(8,128)(2,1)S(1)}, bf16[2,512,512]{2,1,0:T(8,128)(2,1)}, u32[]{:S(2)}) copy-start(bf16[2,512,512]{2,1,0:T(8,128)(2,1)} %constant.25.clone.fx_t) | copy-start | bytes 3145732
Sparse Core Ops, SparseCore 0:
  37.7 128.0 all-reduce.1
where the time goes:
time: 175 us
  waiting for transfers between devices  120 us (69%)
  Pallas kernels  33.4 us (19%)
  between operations  16 us (9%)
  local copies, waits for them, and re-layouts  5.8 us (3%)
    psum x1, waiting for transfers between devices, local(): probe_total = lax.psum(probe_grad, ('angle', 'gz'))  120 us
    pallas_call x1, Pallas kernels, local(): pl.pallas_call(functools.partial(window_kernel, modes), out_shape=(jax.Sh...  21.2 us
    pallas_call x1, Pallas kernels, local(): pl.pallas_call(back_kernel, grid_spec=pltpu.PrefetchScalarGridSpec(num_sc...  8.59 us
    unnamed x17, local copies, waits for them, and re-layouts  5.8 us
    pallas_call x1, Pallas kernels, local(): pl.pallas_call(forward_kernel, grid_spec=pltpu.PrefetchScalarGridSpec(num...  3.64 us
  transfers between devices with their start and end apart: 1, of which 1 were waited for; matrix products, arithmetic and copies ran while one was open for 0% of the time, Pallas kernels for 5%

commit v1 on v0

v1 whole, which is shorter than its diff:
```python
import functools
import math

import jax
import jax.numpy as jnp
import numpy as np
from jax import lax
from jax.experimental import pallas as pl
from jax.experimental.pallas import tpu as pltpu
from jax.sharding import PartitionSpec as P

MESH = pl.DeviceIdType.MESH
F32 = jnp.float32
BF16 = jnp.bfloat16
VM = pl.BlockSpec(memory_space=pltpu.VMEM)
SM = pl.BlockSpec(memory_space=pltpu.SMEM)


def split_table(table):
    table = np.asarray(table, np.float32)
    high = table.astype(jnp.bfloat16)
    low = (table - high.astype(np.float32)).astype(jnp.bfloat16)
    return np.stack([high, low])


def split(value):
    high = value.astype(BF16)
    return high, (value - high.astype(F32)).astype(BF16)


def dot(a, b):
    return jnp.dot(a, b, preferred_element_type=F32)


def dot3(a, b):
    return dot(a[0], b[0]) + (dot(a[0], b[1]) + dot(a[1], b[0]))


def packed_forward(n):
    k = np.arange(n // 2)[:, None]
    x = np.arange(n)[None, :]
    turns = 2.0 * np.pi * (k * x % n) / n
    imag = -np.sin(turns)
    imag[0] = np.where(x[0] % 2 == 0, 1.0, -1.0)
    return np.concatenate([np.cos(turns), imag], axis=0)


def wave_tables(n):
    k = np.arange(n // 2)[:, None]
    y = np.arange(n)[None, :]
    turns = 2.0 * np.pi * (k * y % n) / n
    sine = np.sin(turns)
    sine[0] = np.where(y[0] % 2 == 0, 1.0, -1.0)
    return np.stack([np.cos(turns), sine]).astype(np.float32)


def angle_tables(nx, ny, count):
    rot, mix = [], []
    cells_y = np.arange(ny)[None, :] - ny / 2
    cells_x = np.arange(nx)[None, :] - nx / 2
    weight = np.full(nx // 2, 2.0 / nx)
    weight[0] = 1.0 / nx
    for number in range(count):
        theta = math.pi * (number + 0.5) / count - math.pi / 2
        shear_x = -math.tan(theta / 2)
        shear_y = math.sin(theta)
        kx = np.arange(nx // 2)[:, None]
        one = -2.0 * np.pi * kx * shear_x * cells_y / nx
        nyquist_one = 2.0 * np.pi * (nx // 2) * shear_x * cells_y[0] / nx
        sine = np.sin(one)
        sine[0] = np.cos(nyquist_one)
        rot.append(np.stack([np.cos(one), sine]))
        ky = np.arange(ny // 2)[:, None]
        two = -2.0 * np.pi * ky * shear_y * cells_x / ny
        nyquist_two = 2.0 * np.pi * (ny // 2) * shear_y * cells_x[0] / ny
        upper, lower = np.cos(two), np.sin(two)
        lower[0] = np.cos(nyquist_two)
        spectrum = np.fft.rfft(np.concatenate([upper, lower], axis=0), axis=1)
        real = spectrum.real[:, : nx // 2] * weight
        imag = spectrum.imag[:, : nx // 2] * weight
        imag[:, 0] = spectrum.real[:, nx // 2] / nx
        mix.append(np.concatenate([real, imag], axis=1))
    return np.stack(rot).astype(np.float32), np.stack(mix)


def first_row(shape):
    return lax.broadcasted_iota(jnp.int32, shape, 0) == 0


def half_weights(n):
    return jnp.where(first_row((n // 2, 1)), 1.0 / n, 2.0 / n).astype(F32)


def forward_kernel(number, volume_hbm, fx_hbm, rot_hbm, mix_hbm, wave_hbm, out, volume, fx, rot, mix, wave, sems):
    angle = number[0]
    loads = [
        pltpu.make_async_copy(volume_hbm, volume, sems.at[0]),
        pltpu.make_async_copy(fx_hbm, fx, sems.at[1]),
        pltpu.make_async_copy(rot_hbm.at[pl.ds(angle, 1)], rot, sems.at[2]),
        pltpu.make_async_copy(mix_hbm.at[:, pl.ds(angle, 1)], mix, sems.at[3]),
        pltpu.make_async_copy(wave_hbm, wave, sems.at[4]),
    ]
    for load in loads:
        load.start()
    n = volume.shape[1]
    half = n // 2
    loads[0].wait()
    loads[1].wait()
    field = volume[0]
    spec = dot(fx[0], field) + dot(fx[1], field)
    real, imag = spec[:half], spec[half:]
    loads[2].wait()
    top = first_row((half, 1))
    cosine, raw = rot[0, 0], rot[0, 1]
    sine = jnp.where(top, 0.0, raw)
    turned = jnp.concatenate(
        [real * cosine - imag * sine, real * sine + imag * jnp.where(top, raw, cosine)], axis=0
    )
    loads[3].wait()
    beam = dot3((mix[0, 0], mix[1, 0]), split(turned))
    loads[4].wait()
    upper, lower = beam[:half], beam[half:]
    cosine, raw = wave[0], wave[1]
    sine = jnp.where(top, 0.0, raw)
    weight = half_weights(wave.shape[2])
    sum_real = weight * jnp.sum(upper * cosine + lower * sine, axis=1, keepdims=True)
    sum_imag = weight * jnp.sum(
        lower * jnp.where(top, raw, cosine) - upper * sine, axis=1, keepdims=True
    )
    out[...] = jnp.sum(
        sum_real * cosine - sum_imag * jnp.where(top, -raw, raw), axis=0, keepdims=True
    )


def exact_dot(a, b):
    return jnp.dot(a, b, precision=lax.Precision.HIGHEST, preferred_element_type=F32)


def reduce_plan(angles, depth, tiles):
    angle_bits = [("angle", b) for b in range(angles.bit_length() - 1)]
    gz_bits = [("gz", b) for b in range(1, depth.bit_length() - 1)]
    first = [("gz", 0)] + angle_bits + gz_bits
    second = [("gz", 0)] + angle_bits[::-1] + gz_bits[::-1]
    if tiles % (2 * angles * depth) == 0:
        return [first, second]
    return [first]


class Reducer:
    def __init__(self, place, plan, acc, land, total, sems):
        self.place, self.plan, self.acc, self.land, self.total = place, plan, acc, land, total
        self.sems = sems
        count = len(plan)
        self.length = [acc.shape[0] // count] * count
        self.start = [i * self.length[0] for i in range(count)]
        self.offset = [i * self.length[0] for i in range(count)]
        self.stages = len(plan[0])
        self.flying = []

    def partner(self, axis, bit):
        index = self.place[axis]
        mine = lax.rem(index // (1 << bit), 2)
        other = dict(self.place)
        other[axis] = index + (1 - 2 * mine) * (1 << bit)
        return mine, (other["angle"], other["gz"])

    def copy(self, src, dst, stage, stream, device):
        send, recv = self.sems
        made = pltpu.make_async_remote_copy(
            src_ref=src, dst_ref=dst, send_sem=send.at[stage, stream], recv_sem=recv.at[stage, stream],
            device_id=device, device_id_type=MESH,
        )
        made.start()
        return made

    def start_halving(self, stage, i):
        mine, device = self.partner(*self.plan[i][stage])
        size = self.length[i] // 2
        keep = self.start[i] + mine * size
        other = self.start[i] + (1 - mine) * size
        landing = pl.ds(self.offset[i], size)
        made = self.copy(self.acc.at[pl.ds(other, size)], self.land.at[landing], stage, i, device)
        self.flying.append((made, keep, size, landing))

    def start_doubling(self, stage, i):
        mine, device = self.partner(*self.plan[i][2 * self.stages - 1 - stage])
        rows = self.total.at[pl.ds(self.start[i], self.length[i])]
        made = self.copy(rows, rows, stage, i, device)
        self.start[i] = self.start[i] - mine * self.length[i]
        self.length[i] *= 2
        self.flying.append((made,))

    def begin(self):
        self.stage = 0
        for i in range(len(self.plan)):
            self.start_halving(0, i)

    def advance(self):
        flying, self.flying = self.flying, []
        after = self.stage + 1
        for i, (made, *rest) in enumerate(flying):
            made.wait()
            if self.stage < self.stages:
                keep, size, landing = rest
                rows = pl.ds(keep, size)
                into = self.acc if after < self.stages else self.total
                into[rows] = self.acc[rows] + self.land[landing]
                self.start[i], self.length[i] = keep, size
                self.offset[i] += size
            if after < self.stages:
                self.start_halving(after, i)
            elif after < 2 * self.stages:
                self.start_doubling(after, i)
        self.stage = after


def back_columns(j, angle_rows, wave, weights):
    half, width = wave.shape[1], wave.shape[2]
    row = jnp.zeros((1, width), F32)
    for a in range(angle_rows.shape[0]):
        mine = angle_rows[a, :, width : width + 1] == float(j)
        row = row + jnp.where(mine, angle_rows[a, :, 0:width], 0.0)
    cosine, raw = wave[0], wave[1]
    top = first_row((half, 1))
    weight = half_weights(width)
    weights[j, 0] = weight * jnp.sum(row * cosine, axis=1, keepdims=True)
    weights[j, 1] = -weight * jnp.sum(row * jnp.where(top, -raw, raw), axis=1, keepdims=True)


def back_part(j, cols, weights, rot, mix_t, wave, acc):
    in_real, in_imag = weights[j, 0], weights[j, 1]
    cosine, raw = wave[0, :, cols], wave[1, :, cols]
    top = first_row((cosine.shape[0], 1))
    sine = jnp.where(top, 0.0, raw)
    beam = jnp.concatenate(
        [in_real * cosine - in_imag * sine, in_real * sine + in_imag * jnp.where(top, raw, cosine)], axis=0
    )
    turned = dot3((mix_t[0, j], mix_t[1, j]), split(beam))
    kx = turned.shape[0] // 2
    real, imag = turned[:kx], turned[kx:]
    top = first_row((kx, 1))
    cosine, raw = rot[j, 0, :, cols], rot[j, 1, :, cols]
    sine = jnp.where(top, 0.0, raw)
    upper = real * cosine + imag * sine
    lower = imag * jnp.where(top, raw, cosine) - real * sine
    if j > 0:
        upper, lower = acc[:kx, cols] + upper, acc[kx:, cols] + lower
    acc[:kx, cols] = upper
    acc[kx:, cols] = lower


def window_kernel(
    modes, plan, row_off, col_off, number, row, probe_hbm, measured_hbm, turn_hbm, wave_hbm, rot_hbm, mix_hbm, fx_hbm,
    out, probe_out,
    gathered, sent, received, angle_sent, angle_rows, mat, wide, probe, measured, turn, base, thin, weights,
    wave, rot, mix_t, fx_t, field, acc, land, summed,
    gs, gr, rs, rr, as_, ar, tables, reduce_send, reduce_recv,
):
    depth, angles = gathered.shape[0], angle_rows.shape[0]
    width = row.shape[1]
    window = probe.shape[-1]
    half = window // 2
    g, a = lax.axis_index("gz"), lax.axis_index("angle")

    block_rows = fx_t.shape[1]
    early = [
        pltpu.make_async_copy(turn_hbm, turn, tables.at[4]),
        pltpu.make_async_copy(probe_hbm, probe, tables.at[5]),
        pltpu.make_async_copy(measured_hbm, measured, tables.at[6]),
    ]
    for load in early:
        load.start()
    loads = [
        pltpu.make_async_copy(wave_hbm, wave, tables.at[0]),
        pltpu.make_async_copy(rot_hbm, rot, tables.at[1]),
        pltpu.make_async_copy(mix_hbm, mix_t, tables.at[2]),
        pltpu.make_async_copy(fx_hbm.at[:, pl.ds(a * block_rows, block_rows)], fx_t, tables.at[3]),
    ]
    barrier = pltpu.get_barrier_semaphore()
    for d in range(1, depth):
        pl.semaphore_signal(barrier, inc=1, device_id=(a, lax.rem(g + d, depth)), device_id_type=MESH)
    for d in range(1, angles):
        pl.semaphore_signal(barrier, inc=1, device_id=(lax.rem(a + d, angles), g), device_id_type=MESH)
    pl.semaphore_wait(barrier, depth + angles - 2)

    def push(src, dst, send, recv, device):
        return pltpu.make_async_remote_copy(
            src_ref=src, dst_ref=dst, send_sem=send, recv_sem=recv, device_id=device, device_id_type=MESH
        )

    copies = []
    for d in range(1, depth):
        copies.append(push(row, gathered.at[g], gs.at[d], gr.at[d], (a, lax.rem(g + d, depth))))
        copies[-1].start()
    gathered[g] = row[...]
    for load in early:
        load.wait()
    for load in loads:
        load.start()

    row0, col0 = row_off[0, 0], col_off[0, 0]
    iota = lax.broadcasted_iota
    pick = (iota(jnp.int32, (width, window), 0) == iota(jnp.int32, (width, window), 1) + col0).astype(F32)
    pick_t = (iota(jnp.int32, (window, width), 1) == iota(jnp.int32, (window, width), 0) + col0).astype(F32)
    shape = (2 * depth, depth)
    place = (
        iota(jnp.int32, shape, 0) + (half - depth) == iota(jnp.int32, shape, 1) - row0
    ).astype(F32)
    place_t = (
        iota(jnp.int32, shape[::-1], 1) + (half - depth) == iota(jnp.int32, shape[::-1], 0) - row0
    ).astype(F32)
    low, high, band = half - depth, half + depth, 2 * depth
    left, left_t = (turn[0, 0], turn[0, 1]), (turn[1, 0], turn[1, 1])

    def lanes(m):
        return slice(m * window, (m + 1) * window)

    for m in range(modes):
        wide[lanes(m), 0:window] = probe[m, 0]
        wide[lanes(m), window:] = probe[m, 1]
    wide[...] = dot3(split(wide[...]), left_t)
    for m in range(modes):
        mat[0:window, lanes(m)] = wide[lanes(m), 0:window]
        mat[window:, lanes(m)] = wide[lanes(m), window:]
    base[...] = dot3(left, split(mat[...]))
    for copy in copies:
        copy.wait()

    rows = jnp.concatenate([gathered[z] for z in range(depth)], axis=0)
    patch = exact_dot(place, exact_dot(rows, pick))
    obj_real, obj_imag = jnp.cos(patch), jnp.sin(patch)
    for m in range(modes):
        mid_real, mid_imag = probe[m, 0, low:high], probe[m, 1, low:high]
        thin[m * band : (m + 1) * band, 0:window] = mid_real * obj_real - mid_imag * obj_imag - mid_real
        thin[m * band : (m + 1) * band, window:] = mid_real * obj_imag + mid_imag * obj_real - mid_imag
    change = dot3(split(thin[...]), left_t)
    change = jnp.concatenate(
        [
            jnp.concatenate([change[m * band : (m + 1) * band, c : c + window] for m in range(modes)], axis=1)
            for c in (0, window)
        ],
        axis=0,
    )
    near = tuple(
        jnp.concatenate([part[:, low:high], part[:, window + low : window + high]], axis=1) for part in left
    )
    mat[...] = base[...] + dot3(near, split(change))
    intensity = jnp.zeros((window, window), F32)
    for m in range(modes):
        far_real, far_imag = mat[0:window, lanes(m)], mat[window:, lanes(m)]
        intensity += far_real * far_real + far_imag * far_imag
    factor = (1.0 - jnp.sqrt(measured[0, 0] + 1.0) / jnp.sqrt(intensity + 1.0)) / window
    for m in range(modes):
        mat[0:window, lanes(m)] = mat[0:window, lanes(m)] * factor
        mat[window:, lanes(m)] = mat[window:, lanes(m)] * factor
    mat[...] = dot3(left_t, split(mat[...]))
    for m in range(modes):
        wide[lanes(m), 0:window] = mat[0:window, lanes(m)]
        wide[lanes(m), window:] = mat[window:, lanes(m)]
    wide[...] = dot3(split(wide[...]), left)

    tiles = window // 8
    shape = (tiles, 8, window)
    part = (depth // 4, 8, window)
    grad_real = jnp.zeros((band, window), F32)
    grad_imag = jnp.zeros((band, window), F32)
    for m in range(modes):
        first = m * window
        at = 2 * m * tiles
        acc[at : at + tiles] = wide[lanes(m), 0:window].reshape(shape) * 0.0625
        acc[at + tiles : at + 2 * tiles] = wide[lanes(m), window:].reshape(shape) * 0.0625
        middle = slice(first + low, first + high)
        back_real, back_imag = wide[middle, 0:window], wide[middle, window:]
        top_tile, end_tile = at + low // 8, at + high // 8
        acc[top_tile:end_tile] = (obj_real * back_real + obj_imag * back_imag).reshape(part) * 0.0625
        acc[top_tile + tiles : end_tile + tiles] = (
            obj_real * back_imag - obj_imag * back_real
        ).reshape(part) * 0.0625
    reducer = Reducer({"angle": a, "gz": g}, plan, acc, land, summed, (reduce_send, reduce_recv))
    reducer.begin()

    for m in range(modes):
        middle = slice(m * window + low, m * window + high)
        back_real, back_imag = wide[middle, 0:window], wide[middle, window:]
        mid_real, mid_imag = probe[m, 0, low:high], probe[m, 1, low:high]
        grad_real += mid_real * back_real + mid_imag * back_imag
        grad_imag += mid_real * back_imag - mid_imag * back_real
    patch_grad = grad_imag * obj_real - grad_real * obj_imag
    full = exact_dot(exact_dot(place_t, patch_grad), pick_t)
    for z in range(depth):
        sent[z] = full[z : z + 1]
    copies = []
    for d in range(1, depth):
        peer = lax.rem(g + d, depth)
        copies.append(push(sent.at[peer], received.at[g], rs.at[d], rr.at[d], (a, peer)))
        copies[-1].start()
    received[g] = sent[g]
    reducer.advance()
    for copy in copies:
        copy.wait()
    total = received[0]
    for z in range(1, depth):
        total = total + received[z]
    angle_sent[:, 0:width] = total
    angle_sent[:, width:] = jnp.zeros((1, 128), F32) + number[0].astype(F32)
    copies = []
    for d in range(1, angles):
        copies.append(push(angle_sent, angle_rows.at[a], as_.at[d], ar.at[d], (lax.rem(a + d, angles), g)))
        copies[-1].start()
    angle_rows[a] = angle_sent[...]
    for copy in copies:
        copy.wait()
    for load in loads:
        load.wait()

    block = width // 2
    work = []
    for c in range(2):
        cols = slice(c * block, (c + 1) * block)
        for j in range(angles):
            if c == 0:
                work.append(functools.partial(back_columns, j, angle_rows, wave, weights))
            work.append(functools.partial(back_part, j, cols, weights, rot, mix_t, wave, field))

        def finish(cols):
            out[0, :, cols] = 4.0 * dot3((fx_t[0], fx_t[1]), split(field[:, cols]))

        work.append(functools.partial(finish, cols))
    steps = 2 * reducer.stages - 1
    done = 0
    for step in range(steps):
        until = min(len(work), -(-len(work) * (step + 1) // (steps - 1)))
        for task in work[done:until]:
            task()
        done = until
        reducer.advance()
    probe_out[...] = summed[...]


def local(volume, probe, measured, angle_index, row_offset, col_offset):
    _, nx, ny = volume.shape
    modes, _, window, _ = probe.shape
    depth, angles = lax.axis_size("gz"), lax.axis_size("angle")
    rot, mix = angle_tables(nx, ny, angles)
    mix_pair = split_table(mix)
    mix_t_pair = split_table(np.swapaxes(mix, 1, 2))
    fx = packed_forward(nx)
    fx_pair, fx_t_pair = split_table(fx), split_table(fx.T)
    wave = wave_tables(ny)
    turns = 2.0 * np.pi * (np.arange(window)[:, None] * np.arange(window)[None, :] % window) / window
    cosine, sine = np.cos(turns), np.sin(turns)
    left = np.block([[cosine, sine], [-sine, cosine]])
    turn = np.stack([split_table(left), split_table(left.T)])
    big = 60 * 1024 * 1024
    hbm = pl.BlockSpec(memory_space=pl.ANY)

    row = pl.pallas_call(
        forward_kernel,
        in_specs=[SM] + [hbm] * 5,
        out_specs=VM,
        scratch_shapes=[
            pltpu.VMEM((1, nx, ny), BF16),
            pltpu.VMEM(fx_pair.shape, BF16),
            pltpu.VMEM((1, 2, nx // 2, ny), F32),
            pltpu.VMEM((2, 1, ny, nx), BF16),
            pltpu.VMEM(wave.shape, F32),
            pltpu.SemaphoreType.DMA((5,)),
        ],
        out_shape=jax.ShapeDtypeStruct((1, ny), F32),
        compiler_params=pltpu.CompilerParams(vmem_limit_bytes=big),
        name="forward",
    )(angle_index, volume, fx_pair, rot, mix_pair, wave)

    dma = pltpu.SemaphoreType.DMA
    block_rows = nx // angles
    tiles = modes * 2 * window // 8
    plan = reduce_plan(angles, depth, tiles)
    stages = 2 * len(plan[0])
    out, probe_total = pl.pallas_call(
        functools.partial(window_kernel, modes, plan),
        out_shape=(
            jax.ShapeDtypeStruct((1, block_rows, ny), F32),
            jax.ShapeDtypeStruct((tiles, 8, window), F32),
        ),
        in_specs=[SM, SM, SM, VM] + [hbm] * 7,
        out_specs=(VM, VM),
        scratch_shapes=[
            pltpu.VMEM((depth, 1, ny), F32),
            pltpu.VMEM((depth, 1, ny), F32),
            pltpu.VMEM((depth, 1, ny), F32),
            pltpu.VMEM((1, ny + 128), F32),
            pltpu.VMEM((angles, 1, ny + 128), F32),
            pltpu.VMEM((2 * window, modes * window), F32),
            pltpu.VMEM((modes * window, 2 * window), F32),
            pltpu.VMEM(probe.shape, F32),
            pltpu.VMEM(measured.shape, F32),
            pltpu.VMEM(turn.shape, BF16),
            pltpu.VMEM((2 * window, modes * window), F32),
            pltpu.VMEM((modes * 2 * depth, 2 * window), F32),
            pltpu.VMEM((angles, 2, ny // 2, 1), F32),
            pltpu.VMEM(wave.shape, F32),
            pltpu.VMEM(rot.shape, F32),
            pltpu.VMEM(mix_t_pair.shape, BF16),
            pltpu.VMEM((2, block_rows, nx), BF16),
            pltpu.VMEM((nx, ny), F32),
            pltpu.VMEM((tiles, 8, window), F32),
            pltpu.VMEM((tiles, 8, window), F32),
            pltpu.VMEM((tiles, 8, window), F32),
            dma((depth,)), dma((depth,)), dma((depth,)), dma((depth,)), dma((angles,)), dma((angles,)),
            dma((7,)), dma((stages, len(plan))), dma((stages, len(plan))),
        ],
        compiler_params=pltpu.CompilerParams(
            collective_id=0, has_side_effects=True, vmem_limit_bytes=big
        ),
        name="window",
    )(row_offset, col_offset, angle_index, row, probe, measured, turn, wave, rot, mix_t_pair, fx_t_pair)
    return (out, probe_total.reshape(probe.shape))


def solution(mesh):
    return jax.shard_map(
        local,
        mesh=mesh,
        in_specs=(
            P("gz", None, None),
            P(),
            P("angle", "gz", None, None),
            P("angle"),
            P("angle", "gz"),
            P("angle", "gz"),
        ),
        out_specs=(P("gz", "angle", None), P()),
        check_vma=False,
    )
```

time: 175 us -> 59 us (0.34)
  waiting for transfers between devices: 120 us -> 0 us
  Pallas kernels: 33.4 us -> 52.3 us
  between operations: 16 us -> 2.58 us
  local copies, waits for them, and re-layouts: 5.8 us -> 3.97 us
    psum x1 -> x0, waiting for transfers between devices: 120 us -> none  [local(): probe_total = lax.psum(probe_grad, ('angle', 'gz'))]
    pallas_call x3 -> x2, Pallas kernels: 33.4 us -> 52.3 us  [the longest x1 48.1 us: local(): pl.pallas_call(functools.partial(window_kernel, modes, plan), out_shape=(...]
    unnamed x17 -> x2, local copies, waits for them, and re-layouts: 5.8 us -> 3.97 us
  transfers between devices with their start and end apart: 1 -> 0, of which waited for: 1 -> 0; matrix products, arithmetic and copies ran while one was open for 0% -> 0% of each run, Pallas kernels for 5% -> 0%
where the time goes in v1:
time: 59 us; the launch traced here: 58.8 us
  Pallas kernels  52.3 us (89%)
  local copies, waits for them, and re-layouts  3.97 us (7%)
  between operations  2.58 us (4%)
    pallas_call x1, Pallas kernels, local(): pl.pallas_call(functools.partial(window_kernel, modes, plan), out_shape=(...  48.1 us
    pallas_call x1, Pallas kernels, local(): pl.pallas_call(forward_kernel, in_specs=[SM] + [hbm] * 5, out_specs=VM, s...  4.2 us
    unnamed x2, local copies, waits for them, and re-layouts  3.97 us

profile of v1, /device:TPU:0, one launch (start us, length us, event | category | flops | bytes accessed | tf_op | source)
XLA Modules:
  0.0 58.8 jit_solution(10305104624108535039)
XLA Ops:
  2.6 4.2 %forward.1.row = f32[1,512]{1,0:T(1,128)} custom-call(s32[1]{0:T(128)S(6)} %copy.17.number, bf16[1,512,512]{2,1,0:T(8,128)(2,1)} %volume_hbm.1, bf16[2,512,512]{2,1,0:T(8,128)(2,1)} %constant.14.clone.fx_hbm, f32[4,2,256,512]{3,2,1,0:T(8,128)} %constant.15.clone.rot_hbm, bf16[2,4,512,512]{3,2,1,0:T(8,128)(2,1)} %constant.16.clone.mix_hbm, ...), custom_call_target="tpu_custom_call" | custom-call | tf_op jit(solution)/shard_map/forward/pallas_call | solution.py:457
  6.8 48.1 %window.1 = (f32[1,128,512]{2,1,0:T(8,128)}, f32[256,8,128]{2,1,0:T(8,128)}) custom-call(s32[1,1]{1,0:T(1,128)S(6)} %copy.18.row_off, s32[1,1]{1,0:T(1,128)S(6)} %copy.19.col_off, s32[1]{0:T(128)S(6)} %copy.17.number, f32[1,512]{1,0:T(1,128)} %forward.1.row, f32[8,2,128,128]{3,2,1,0:T(8,128)} %probe_hbm.1, f32[1,1,128,128]{3,2,1,0:T(8,128)} %measured_hbm.1, ...), custom_call_target="tpu_custom_call" | custom-call | tf_op jit(solution)/shard_map/window/pallas_call | solution.py:479
  54.8 1.7 %copy.20 = f32[1,128,512]{2,1,0:T(8,128)} copy(f32[1,128,512]{2,1,0:T(8,128)} %get-tuple-element.8) | data formatting | bytes 524288
  56.5 2.3 %copy.21 = f32[8,2,128,128]{3,2,1,0:T(8,128)} copy(f32[8,2,128,128]{3,2,1,0:T(8,128)} %bitcast.1) | data formatting | bytes 2097152

commit v2 on v1

--- a/solution.py
+++ b/solution.py
@@ -139,22 +139,29 @@
 def reduce_plan(angles, depth, tiles):
     angle_bits = [("angle", b) for b in range(angles.bit_length() - 1)]
     gz_bits = [("gz", b) for b in range(1, depth.bit_length() - 1)]
-    first = [("gz", 0)] + angle_bits + gz_bits
-    second = [("gz", 0)] + angle_bits[::-1] + gz_bits[::-1]
-    if tiles % (2 * angles * depth) == 0:
-        return [first, second]
-    return [first]
+    core = [("gz", 0)]
+    along_x = core + angle_bits + gz_bits
+    along_y = core + angle_bits[::-1] + gz_bits
+    z_then_x = core + gz_bits + angle_bits
+    z_then_y = core + gz_bits + angle_bits[::-1]
+    unit = angles * depth
+    if tiles != 8 * unit:
+        return [(along_x, tiles)]
+    return [
+        (along_x, 2 * unit), (along_y, 2 * unit), (z_then_x, unit),
+        (z_then_y, unit), (along_x, unit), (along_y, unit),
+    ]
 
 
 class Reducer:
     def __init__(self, place, plan, acc, land, total, sems):
-        self.place, self.plan, self.acc, self.land, self.total = place, plan, acc, land, total
+        self.place, self.acc, self.land, self.total = place, acc, land, total
         self.sems = sems
-        count = len(plan)
-        self.length = [acc.shape[0] // count] * count
-        self.start = [i * self.length[0] for i in range(count)]
-        self.offset = [i * self.length[0] for i in range(count)]
-        self.stages = len(plan[0])
+        self.plan = [order for order, _ in plan]
+        self.length = [size for _, size in plan]
+        self.start = [sum(self.length[:i]) for i in range(len(plan))]
+        self.offset = list(self.start)
+        self.stages = len(self.plan[0])
         self.flying = []
 
     def partner(self, axis, bit):
@@ -475,7 +482,7 @@
     block_rows = nx // angles
     tiles = modes * 2 * window // 8
     plan = reduce_plan(angles, depth, tiles)
-    stages = 2 * len(plan[0])
+    stages = 2 * len(plan[0][0])
     out, probe_total = pl.pallas_call(
         functools.partial(window_kernel, modes, plan),
         out_shape=(
@@ -510,7 +517,7 @@
             dma((7,)), dma((stages, len(plan))), dma((stages, len(plan))),
         ],
         compiler_params=pltpu.CompilerParams(
-            collective_id=0, has_side_effects=True, vmem_limit_bytes=big
+            collective_id=0, has_side_effects=True, vmem_limit_bytes=48 * 1024 * 1024
         ),
         name="window",
     )(row_offset, col_offset, angle_index, row, probe, measured, turn, wave, rot, mix_t_pair, fx_t_pair)

time: 59 us -> 55 us (0.932)
  Pallas kernels: 52.3 us -> 49.7 us
  local copies, waits for them, and re-layouts: 3.97 us -> 2.38 us
    pallas_call x1, Pallas kernels: 48.1 us -> 45.4 us  [local(): pl.pallas_call(functools.partial(window_kernel, modes, plan), out_shape=(...]
    unnamed x2 -> x14, local copies, waits for them, and re-layouts: 3.97 us -> 2.38 us
where the time goes in v2:
time: 55 us; the launch traced here: 54.8 us
  Pallas kernels  49.7 us (90%)
  between operations  2.67 us (5%)
  local copies, waits for them, and re-layouts  2.38 us (4%)
    pallas_call x1, Pallas kernels, local(): pl.pallas_call(functools.partial(window_kernel, modes, plan), out_shape=(...  45.4 us
    pallas_call x1, Pallas kernels, local(): pl.pallas_call(forward_kernel, in_specs=[SM] + [hbm] * 5, out_specs=VM, s...  4.34 us
    unnamed x14, local copies, waits for them, and re-layouts  2.38 us

profile of v2, /device:TPU:0, one launch (start us, length us, event | category | flops | bytes accessed | tf_op | source)
XLA Modules:
  0.0 54.8 jit_solution(18401010790701577050)
XLA Ops:
  2.6 0.0 copy-start
  2.6 0.0 copy-start.1
  2.6 0.0 copy-start.2
  2.6 0.0 copy-start.3
  2.6 0.0 copy-start.4
  2.6 4.3 %forward.1.row = f32[1,512]{1,0:T(1,128)} custom-call(s32[1]{0:T(128)S(6)} %copy.17.number, bf16[1,512,512]{2,1,0:T(8,128)(2,1)} %volume_hbm.1, bf16[2,512,512]{2,1,0:T(8,128)(2,1)} %constant.14.clone.fx_hbm, f32[4,2,256,512]{3,2,1,0:T(8,128)} %constant.15.clone.rot_hbm, bf16[2,4,512,512]{3,2,1,0:T(8,128)(2,1)} %constant.16.clone.mix_hbm, ...), custom_call_target="tpu_custom_call" | custom-call | tf_op jit(solution)/shard_map/forward/pallas_call | solution.py:464
  7.0 0.0 copy-done
  7.0 0.0 copy-done.1
  7.0 0.0 copy-done.2
  7.0 0.0 copy-done.3
  7.0 0.0 copy-done.4
  7.0 0.0 copy-start.5
  7.0 0.7 %copy-done.5 = f32[1,512]{1,0:T(1,128)S(1)} copy-done((f32[1,512]{1,0:T(1,128)S(1)}, f32[1,512]{1,0:T(1,128)}, u32[]{:S(2)}) %copy-start.5) | copy-done | bytes 2072
  7.7 45.4 %window.1 = (f32[1,128,512]{2,1,0:T(8,128)S(1)}, f32[256,8,128]{2,1,0:T(8,128)S(1)}) custom-call(s32[1,1]{1,0:T(1,128)S(6)} %copy.18.row_off, s32[1,1]{1,0:T(1,128)S(6)} %copy.19.col_off, s32[1]{0:T(128)S(6)} %copy.17.number, f32[1,512]{1,0:T(1,128)S(1)} %copy-done.5, f32[8,2,128,128]{3,2,1,0:T(8,128)S(1)} %copy-done.1, f32[1,1,128,128]{3,2,1,0:T(8,128)S(1)} %copy-done.4, ...), custom_call_target="tpu_custom_call" | custom-call | tf_op jit(solution)/shard_map/window/pallas_call | solution.py:486
  53.1 0.7 %copy.20 = f32[1,128,512]{2,1,0:T(8,128)} copy(f32[1,128,512]{2,1,0:T(8,128)S(1)} %get-tuple-element.8) | data formatting | bytes 524288
  53.8 1.0 %copy.21 = f32[8,2,128,128]{3,2,1,0:T(8,128)} copy(f32[8,2,128,128]{3,2,1,0:T(8,128)S(1)} %bitcast.1) | data formatting | bytes 2097152
Async XLA Ops:
  2.6 4.4 %copy-start = (f32[2,256,512]{2,1,0:T(8,128)S(1)}, f32[2,256,512]{2,1,0:T(8,128)}, u32[]{:S(2)}) copy-start(f32[2,256,512]{2,1,0:T(8,128)} %constant.17.clone.wave_hbm) | copy-start | bytes 3145732
  2.6 4.4 %copy-start.1 = (f32[8,2,128,128]{3,2,1,0:T(8,128)S(1)}, f32[8,2,128,128]{3,2,1,0:T(8,128)}, u32[]{:S(2)}) copy-start(f32[8,2,128,128]{3,2,1,0:T(8,128)} %probe_hbm.1) | copy-start | bytes 3145732
  2.6 4.4 %copy-start.2 = (bf16[2,512,512]{2,1,0:T(8,128)(2,1)S(1)}, bf16[2,512,512]{2,1,0:T(8,128)(2,1)}, u32[]{:S(2)}) copy-start(bf16[2,512,512]{2,1,0:T(8,128)(2,1)} %constant.20.clone.fx_hbm) | copy-start | bytes 3145732
  2.6 4.4 %copy-start.3 = (bf16[2,2,256,256]{3,2,1,0:T(8,128)(2,1)S(1)}, bf16[2,2,256,256]{3,2,1,0:T(8,128)(2,1)}, u32[]{:S(2)}) copy-start(bf16[2,2,256,256]{3,2,1,0:T(8,128)(2,1)} %constant.18.clone.turn_hbm) | copy-start | bytes 1572868
  2.6 4.4 %copy-start.4 = (f32[1,1,128,128]{3,2,1,0:T(8,128)S(1)}, f32[1,1,128,128]{3,2,1,0:T(8,128)}, u32[]{:S(2)}) copy-start(f32[1,1,128,128]{3,2,1,0:T(8,128)} %measured_hbm.1) | copy-start | bytes 196612
  7.0 0.7 %copy-start.5 = (f32[1,512]{1,0:T(1,128)S(1)}, f32[1,512]{1,0:T(1,128)}, u32[]{:S(2)}) copy-start(f32[1,512]{1,0:T(1,128)} %forward.1.row) | copy-start | bytes 6148

commit v3 on v2

--- a/solution.py
+++ b/solution.py
@@ -45,13 +45,33 @@
     return np.concatenate([np.cos(turns), imag], axis=0)
 
 
+FINE = 16
+
+
+def phase_table(unit, nyquist, count):
+    rows = np.arange(FINE)[:, None]
+    coarse = np.arange(count // 2 // FINE)[:, None] * FINE
+    table = np.zeros((5, max(FINE, coarse.shape[0]), unit.shape[0]))
+    for at, steps in ((0, coarse), (2, rows)):
+        table[at, : len(steps)] = np.cos(steps * unit)
+        table[at + 1, : len(steps)] = np.sin(steps * unit)
+    table[4, 0] = nyquist
+    return table.astype(np.float32)
+
+
+def expand(small, full):
+    fine_cos, fine_sin = small[2, 0:FINE], small[3, 0:FINE]
+    for a in range(full.shape[1] // FINE):
+        coarse_cos, coarse_sin = small[0, a : a + 1], small[1, a : a + 1]
+        rows = slice(a * FINE, (a + 1) * FINE)
+        full[0, rows] = coarse_cos * fine_cos - coarse_sin * fine_sin
+        full[1, rows] = coarse_sin * fine_cos + coarse_cos * fine_sin
+    full[1, 0:1] = small[4, 0:1]
+
+
 def wave_tables(n):
-    k = np.arange(n // 2)[:, None]
-    y = np.arange(n)[None, :]
-    turns = 2.0 * np.pi * (k * y % n) / n
-    sine = np.sin(turns)
-    sine[0] = np.where(y[0] % 2 == 0, 1.0, -1.0)
-    return np.stack([np.cos(turns), sine]).astype(np.float32)
+    y = np.arange(n)
+    return phase_table(2.0 * np.pi * y / n, np.where(y % 2 == 0, 1.0, -1.0), n)
 
 
 def angle_tables(nx, ny, count):
@@ -64,12 +84,8 @@
         theta = math.pi * (number + 0.5) / count - math.pi / 2
         shear_x = -math.tan(theta / 2)
         shear_y = math.sin(theta)
-        kx = np.arange(nx // 2)[:, None]
-        one = -2.0 * np.pi * kx * shear_x * cells_y / nx
-        nyquist_one = 2.0 * np.pi * (nx // 2) * shear_x * cells_y[0] / nx
-        sine = np.sin(one)
-        sine[0] = np.cos(nyquist_one)
-        rot.append(np.stack([np.cos(one), sine]))
+        unit = -2.0 * np.pi * shear_x * cells_y[0] / nx
+        rot.append(phase_table(unit, np.cos(unit * (nx // 2)), nx))
         ky = np.arange(ny // 2)[:, None]
         two = -2.0 * np.pi * ky * shear_y * cells_x / ny
         nyquist_two = 2.0 * np.pi * (ny // 2) * shear_y * cells_x[0] / ny
@@ -80,7 +96,7 @@
         imag = spectrum.imag[:, : nx // 2] * weight
         imag[:, 0] = spectrum.real[:, nx // 2] / nx
         mix.append(np.concatenate([real, imag], axis=1))
-    return np.stack(rot).astype(np.float32), np.stack(mix)
+    return np.stack(rot), np.stack(mix)
 
 
 def first_row(shape):
@@ -91,25 +107,28 @@
     return jnp.where(first_row((n // 2, 1)), 1.0 / n, 2.0 / n).astype(F32)
 
 
-def forward_kernel(number, volume_hbm, fx_hbm, rot_hbm, mix_hbm, wave_hbm, out, volume, fx, rot, mix, wave, sems):
+def forward_kernel(number, volume_hbm, fx_hbm, rot_hbm, mix_hbm, wave_hbm, out, volume, fx, rot_small, mix, wave_small, rot, wave, sems):
     angle = number[0]
     loads = [
         pltpu.make_async_copy(volume_hbm, volume, sems.at[0]),
         pltpu.make_async_copy(fx_hbm, fx, sems.at[1]),
-        pltpu.make_async_copy(rot_hbm.at[pl.ds(angle, 1)], rot, sems.at[2]),
+        pltpu.make_async_copy(rot_hbm.at[pl.ds(angle, 1)], rot_small, sems.at[2]),
         pltpu.make_async_copy(mix_hbm.at[:, pl.ds(angle, 1)], mix, sems.at[3]),
-        pltpu.make_async_copy(wave_hbm, wave, sems.at[4]),
+        pltpu.make_async_copy(wave_hbm, wave_small, sems.at[4]),
     ]
-    for load in loads:
-        load.start()
+    for at in (2, 4, 0, 1, 3):
+        loads[at].start()
     n = volume.shape[1]
     half = n // 2
+    loads[2].wait()
+    expand(rot_small.at[0], rot.at[0])
+    loads[4].wait()
+    expand(wave_small, wave)
     loads[0].wait()
     loads[1].wait()
     field = volume[0]
     spec = dot(fx[0], field) + dot(fx[1], field)
     real, imag = spec[:half], spec[half:]
-    loads[2].wait()
     top = first_row((half, 1))
     cosine, raw = rot[0, 0], rot[0, 1]
     sine = jnp.where(top, 0.0, raw)
@@ -118,7 +137,6 @@
     )
     loads[3].wait()
     beam = dot3((mix[0, 0], mix[1, 0]), split(turned))
-    loads[4].wait()
     upper, lower = beam[:half], beam[half:]
     cosine, raw = wave[0], wave[1]
     sine = jnp.where(top, 0.0, raw)
@@ -221,7 +239,9 @@
         self.stage = after
 
 
-def back_columns(j, angle_rows, wave, weights):
+def back_columns(j, angle_rows, wave, weights, rot_small, rot):
+    if j > 0:
+        expand(rot_small.at[j], rot.at[j])
     half, width = wave.shape[1], wave.shape[2]
     row = jnp.zeros((1, width), F32)
     for a in range(angle_rows.shape[0]):
@@ -259,7 +279,7 @@
 def window_kernel(
     modes, plan, row_off, col_off, number, row, probe_hbm, measured_hbm, turn_hbm, wave_hbm, rot_hbm, mix_hbm, fx_hbm,
     out, probe_out,
-    gathered, sent, received, angle_sent, angle_rows, mat, wide, probe, measured, turn, base, thin, weights,
+    gathered, sent, received, angle_sent, angle_rows, mat, wide, probe, measured, turn, base, thin, weights, wave_small, rot_small,
     wave, rot, mix_t, fx_t, field, acc, land, summed,
     gs, gr, rs, rr, as_, ar, tables, reduce_send, reduce_recv,
 ):
@@ -278,8 +298,8 @@
     for load in early:
         load.start()
     loads = [
-        pltpu.make_async_copy(wave_hbm, wave, tables.at[0]),
-        pltpu.make_async_copy(rot_hbm, rot, tables.at[1]),
+        pltpu.make_async_copy(wave_hbm, wave_small, tables.at[0]),
+        pltpu.make_async_copy(rot_hbm, rot_small, tables.at[1]),
         pltpu.make_async_copy(mix_hbm, mix_t, tables.at[2]),
         pltpu.make_async_copy(fx_hbm.at[:, pl.ds(a * block_rows, block_rows)], fx_t, tables.at[3]),
     ]
@@ -402,7 +422,10 @@
         copies.append(push(sent.at[peer], received.at[g], rs.at[d], rr.at[d], (a, peer)))
         copies[-1].start()
     received[g] = sent[g]
+    for load in loads:
+        load.wait()
     reducer.advance()
+    expand(wave_small, wave)
     for copy in copies:
         copy.wait()
     total = received[0]
@@ -415,10 +438,10 @@
         copies.append(push(angle_sent, angle_rows.at[a], as_.at[d], ar.at[d], (lax.rem(a + d, angles), g)))
         copies[-1].start()
     angle_rows[a] = angle_sent[...]
+    expand(rot_small.at[0], rot.at[0])
+    reducer.advance()
     for copy in copies:
         copy.wait()
-    for load in loads:
-        load.wait()
 
     block = width // 2
     work = []
@@ -426,17 +449,20 @@
         cols = slice(c * block, (c + 1) * block)
         for j in range(angles):
             if c == 0:
-                work.append(functools.partial(back_columns, j, angle_rows, wave, weights))
+                work.append(functools.partial(back_columns, j, angle_rows, wave, weights, rot_small, rot))
             work.append(functools.partial(back_part, j, cols, weights, rot, mix_t, wave, field))
 
         def finish(cols):
             out[0, :, cols] = 4.0 * dot3((fx_t[0], fx_t[1]), split(field[:, cols]))
 
         work.append(functools.partial(finish, cols))
-    steps = 2 * reducer.stages - 1
+    steps = 2 * reducer.stages - 2
+    share = [1] * steps
+    share[0] = share[-3] = 3
+    share[-2], share[-1] = 4, 0
     done = 0
     for step in range(steps):
-        until = min(len(work), -(-len(work) * (step + 1) // (steps - 1)))
+        until = -(-len(work) * sum(share[: step + 1]) // sum(share))
         for task in work[done:until]:
             task()
         done = until
@@ -468,9 +494,11 @@
         scratch_shapes=[
             pltpu.VMEM((1, nx, ny), BF16),
             pltpu.VMEM(fx_pair.shape, BF16),
-            pltpu.VMEM((1, 2, nx // 2, ny), F32),
+            pltpu.VMEM((1,) + rot.shape[1:], F32),
             pltpu.VMEM((2, 1, ny, nx), BF16),
             pltpu.VMEM(wave.shape, F32),
+            pltpu.VMEM((1, 2, nx // 2, ny), F32),
+            pltpu.VMEM((2, ny // 2, ny), F32),
             pltpu.SemaphoreType.DMA((5,)),
         ],
         out_shape=jax.ShapeDtypeStruct((1, ny), F32),
@@ -507,6 +535,8 @@
             pltpu.VMEM((angles, 2, ny // 2, 1), F32),
             pltpu.VMEM(wave.shape, F32),
             pltpu.VMEM(rot.shape, F32),
+            pltpu.VMEM((2, ny // 2, ny), F32),
+            pltpu.VMEM((angles, 2, nx // 2, ny), F32),
             pltpu.VMEM(mix_t_pair.shape, BF16),
             pltpu.VMEM((2, block_rows, nx), BF16),
             pltpu.VMEM((nx, ny), F32),

time: 55 us -> 52.5 us (0.955)
  Pallas kernels: 49.7 us -> 46.9 us
    pallas_call x1, Pallas kernels: 45.4 us -> 42.7 us  [local(): pl.pallas_call(functools.partial(window_kernel, modes, plan), out_shape=(...]
    unnamed x14 -> x16, local copies, waits for them, and re-layouts: 2.38 us -> 2.39 us
where the time goes in v3:
time: 52.5 us; the launch traced here: 52.3 us
  Pallas kernels  46.9 us (89%)
  between operations  3.08 us (6%)
  local copies, waits for them, and re-layouts  2.39 us (5%)
    pallas_call x1, Pallas kernels, local(): pl.pallas_call(functools.partial(window_kernel, modes, plan), out_shape=(...  42.7 us
    pallas_call x1, Pallas kernels, local(): pl.pallas_call(forward_kernel, in_specs=[SM] + [hbm] * 5, out_specs=VM, s...  4.13 us
    unnamed x16, local copies, waits for them, and re-layouts  2.39 us

profile of v3, /device:TPU:0, one launch (start us, length us, event | category | flops | bytes accessed | tf_op | source)
XLA Modules:
  0.0 52.3 jit_solution(3651669955737016921)
XLA Ops:
  0.6 0.0 copy-start.3
  0.6 0.0 copy-start
  0.7 0.0 copy-start.2
  0.7 0.0 copy-start.4
  0.7 0.0 copy-start.5
  0.7 0.0 copy-start.1
  3.0 4.1 %forward.1.row = f32[1,512]{1,0:T(1,128)} custom-call(s32[1]{0:T(128)S(6)} %copy.17.number, bf16[1,512,512]{2,1,0:T(8,128)(2,1)} %volume_hbm.1, bf16[2,512,512]{2,1,0:T(8,128)(2,1)} %constant.14.clone.fx_hbm, f32[4,5,16,512]{3,2,1,0:T(8,128)} %constant.15.clone.rot_hbm, bf16[2,4,512,512]{3,2,1,0:T(8,128)(2,1)} %constant.16.clone.mix_hbm, ...), custom_call_target="tpu_custom_call" | custom-call | tf_op jit(solution)/shard_map/forward/pallas_call | solution.py:490
  7.2 0.0 copy-done.3
  7.2 0.0 copy-done
  7.2 0.0 copy-done.2
  7.2 0.0 copy-done.4
  7.2 0.0 copy-done.5
  7.2 0.0 copy-done.1
  7.2 0.0 copy-start.6
  7.2 0.7 %copy-done.6 = f32[1,512]{1,0:T(1,128)S(1)} copy-done((f32[1,512]{1,0:T(1,128)S(1)}, f32[1,512]{1,0:T(1,128)}, u32[]{:S(2)}) %copy-start.6) | copy-done | bytes 2072
  7.9 42.7 %window.1 = (f32[1,128,512]{2,1,0:T(8,128)S(1)}, f32[256,8,128]{2,1,0:T(8,128)S(1)}) custom-call(s32[1,1]{1,0:T(1,128)S(6)} %copy.18.row_off, s32[1,1]{1,0:T(1,128)S(6)} %copy.19.col_off, s32[1]{0:T(128)S(6)} %copy.17.number, f32[1,512]{1,0:T(1,128)S(1)} %copy-done.6, f32[8,2,128,128]{3,2,1,0:T(8,128)S(1)} %copy-done.1, f32[1,1,128,128]{3,2,1,0:T(8,128)S(1)} %copy-done.5, ...), custom_call_target="tpu_custom_call" | custom-call | tf_op jit(solution)/shard_map/window/pallas_call | solution.py:514
  50.6 0.7 %copy.20 = f32[1,128,512]{2,1,0:T(8,128)} copy(f32[1,128,512]{2,1,0:T(8,128)S(1)} %get-tuple-element.8) | data formatting | bytes 524288
  51.4 1.0 %copy.21 = f32[8,2,128,128]{3,2,1,0:T(8,128)} copy(f32[8,2,128,128]{3,2,1,0:T(8,128)S(1)} %bitcast.1) | data formatting | bytes 2097152
Async XLA Ops:
  0.6 6.5 %copy-start.3 = (f32[5,16,512]{2,1,0:T(8,128)S(1)}, f32[5,16,512]{2,1,0:T(8,128)}, u32[]{:S(2)}) copy-start(f32[5,16,512]{2,1,0:T(8,128)} %constant.17.clone.wave_hbm) | copy-start | bytes 491524
  0.6 6.5 %copy-start = (f32[4,5,16,512]{3,2,1,0:T(8,128)S(1)}, f32[4,5,16,512]{3,2,1,0:T(8,128)}, u32[]{:S(2)}) copy-start(f32[4,5,16,512]{3,2,1,0:T(8,128)} %constant.15.clone.rot_hbm) | copy-start | bytes 1966084
  0.7 6.5 %copy-start.2 = (bf16[2,512,512]{2,1,0:T(8,128)(2,1)S(1)}, bf16[2,512,512]{2,1,0:T(8,128)(2,1)}, u32[]{:S(2)}) copy-start(bf16[2,512,512]{2,1,0:T(8,128)(2,1)} %constant.20.clone.fx_hbm) | copy-start | bytes 3145732
  0.7 6.5 %copy-start.4 = (bf16[2,2,256,256]{3,2,1,0:T(8,128)(2,1)S(1)}, bf16[2,2,256,256]{3,2,1,0:T(8,128)(2,1)}, u32[]{:S(2)}) copy-start(bf16[2,2,256,256]{3,2,1,0:T(8,128)(2,1)} %constant.18.clone.turn_hbm) | copy-start | bytes 1572868
  0.7 6.5 %copy-start.5 = (f32[1,1,128,128]{3,2,1,0:T(8,128)S(1)}, f32[1,1,128,128]{3,2,1,0:T(8,128)}, u32[]{:S(2)}) copy-start(f32[1,1,128,128]{3,2,1,0:T(8,128)} %measured_hbm.1) | copy-start | bytes 196612
  0.7 6.5 %copy-start.1 = (f32[8,2,128,128]{3,2,1,0:T(8,128)S(1)}, f32[8,2,128,128]{3,2,1,0:T(8,128)}, u32[]{:S(2)}) copy-start(f32[8,2,128,128]{3,2,1,0:T(8,128)} %probe_hbm.1) | copy-start | bytes 3145732
  7.2 0.7 %copy-start.6 = (f32[1,512]{1,0:T(1,128)S(1)}, f32[1,512]{1,0:T(1,128)}, u32[]{:S(2)}) copy-start(f32[1,512]{1,0:T(1,128)} %forward.1.row) | copy-start | bytes 6148

commit v4 on v3

--- a/solution.py
+++ b/solution.py
@@ -155,13 +155,13 @@
 
 
 def reduce_plan(angles, depth, tiles):
-    angle_bits = [("angle", b) for b in range(angles.bit_length() - 1)]
-    gz_bits = [("gz", b) for b in range(1, depth.bit_length() - 1)]
-    core = [("gz", 0)]
-    along_x = core + angle_bits + gz_bits
-    along_y = core + angle_bits[::-1] + gz_bits
-    z_then_x = core + gz_bits + angle_bits
-    z_then_y = core + gz_bits + angle_bits[::-1]
+    angle_bits = [("angle", 1 << b, 2) for b in range(angles.bit_length() - 1)]
+    core = [("gz", 1, 2)]
+    along_z = [("gz", 2, 4)] + [("gz", 1 << b, 2) for b in range(3, depth.bit_length() - 1)]
+    along_x = core + angle_bits + along_z
+    along_y = core + angle_bits[::-1] + along_z
+    z_then_x = core + along_z + angle_bits
+    z_then_y = core + along_z + angle_bits[::-1]
     unit = angles * depth
     if tiles != 8 * unit:
         return [(along_x, tiles)]
@@ -182,37 +182,48 @@
         self.stages = len(self.plan[0])
         self.flying = []
 
-    def partner(self, axis, bit):
+    def partners(self, axis, unit, ways):
         index = self.place[axis]
-        mine = lax.rem(index // (1 << bit), 2)
-        other = dict(self.place)
-        other[axis] = index + (1 - 2 * mine) * (1 << bit)
-        return mine, (other["angle"], other["gz"])
-
-    def copy(self, src, dst, stage, stream, device):
+        mine = lax.rem(index // unit, ways)
+        found = []
+        for mask in range(1, ways):
+            piece = 0
+            for b in range(ways.bit_length() - 1):
+                bit = lax.rem(mine // (1 << b), 2)
+                piece = piece + (1 << b) * (1 - bit if mask >> b & 1 else bit)
+            other = dict(self.place)
+            other[axis] = index + (piece - mine) * unit
+            found.append((piece, (other["angle"], other["gz"])))
+        return mine, found
+
+    def copy(self, src, dst, stage, stream, lane, device):
         send, recv = self.sems
         made = pltpu.make_async_remote_copy(
-            src_ref=src, dst_ref=dst, send_sem=send.at[stage, stream], recv_sem=recv.at[stage, stream],
+            src_ref=src, dst_ref=dst, send_sem=send.at[stage, stream, lane], recv_sem=recv.at[stage, stream, lane],
             device_id=device, device_id_type=MESH,
         )
         made.start()
         return made
 
     def start_halving(self, stage, i):
-        mine, device = self.partner(*self.plan[i][stage])
-        size = self.length[i] // 2
-        keep = self.start[i] + mine * size
-        other = self.start[i] + (1 - mine) * size
-        landing = pl.ds(self.offset[i], size)
-        made = self.copy(self.acc.at[pl.ds(other, size)], self.land.at[landing], stage, i, device)
-        self.flying.append((made, keep, size, landing))
+        ways = self.plan[i][stage][2]
+        mine, found = self.partners(*self.plan[i][stage])
+        size = self.length[i] // ways
+        made, landings = [], []
+        for lane, (piece, device) in enumerate(found):
+            landing = pl.ds(self.offset[i] + lane * size, size)
+            other = pl.ds(self.start[i] + piece * size, size)
+            made.append(self.copy(self.acc.at[other], self.land.at[landing], stage, i, lane, device))
+            landings.append(landing)
+        self.flying.append((made, self.start[i] + mine * size, size, landings))
 
     def start_doubling(self, stage, i):
-        mine, device = self.partner(*self.plan[i][2 * self.stages - 1 - stage])
+        step = self.plan[i][2 * self.stages - 1 - stage]
+        mine, found = self.partners(*step)
         rows = self.total.at[pl.ds(self.start[i], self.length[i])]
-        made = self.copy(rows, rows, stage, i, device)
+        made = [self.copy(rows, rows, stage, i, lane, device) for lane, (_, device) in enumerate(found)]
         self.start[i] = self.start[i] - mine * self.length[i]
-        self.length[i] *= 2
+        self.length[i] *= step[2]
         self.flying.append((made,))
 
     def begin(self):
@@ -224,14 +235,18 @@
         flying, self.flying = self.flying, []
         after = self.stage + 1
         for i, (made, *rest) in enumerate(flying):
-            made.wait()
+            for one in made:
+                one.wait()
             if self.stage < self.stages:
-                keep, size, landing = rest
+                keep, size, landings = rest
                 rows = pl.ds(keep, size)
                 into = self.acc if after < self.stages else self.total
-                into[rows] = self.acc[rows] + self.land[landing]
+                value = self.acc[rows]
+                for landing in landings:
+                    value = value + self.land[landing]
+                into[rows] = value
                 self.start[i], self.length[i] = keep, size
-                self.offset[i] += size
+                self.offset[i] += size * len(landings)
             if after < self.stages:
                 self.start_halving(after, i)
             elif after < 2 * self.stages:
@@ -544,7 +559,7 @@
             pltpu.VMEM((tiles, 8, window), F32),
             pltpu.VMEM((tiles, 8, window), F32),
             dma((depth,)), dma((depth,)), dma((depth,)), dma((depth,)), dma((angles,)), dma((angles,)),
-            dma((7,)), dma((stages, len(plan))), dma((stages, len(plan))),
+            dma((7,)), dma((stages, len(plan), 3)), dma((stages, len(plan), 3)),
         ],
         compiler_params=pltpu.CompilerParams(
             collective_id=0, has_side_effects=True, vmem_limit_bytes=48 * 1024 * 1024

time: 52.5 us -> 50.6 us (0.964)
  Pallas kernels: 46.9 us -> 44.9 us
    pallas_call x1, Pallas kernels: 42.7 us -> 40.8 us  [local(): pl.pallas_call(functools.partial(window_kernel, modes, plan), out_shape=(...]
where the time goes in v4:
time: 50.6 us; the launch traced here: 50.4 us
  Pallas kernels  44.9 us (89%)
  between operations  3.08 us (6%)
  local copies, waits for them, and re-layouts  2.39 us (5%)
    pallas_call x1, Pallas kernels, local(): pl.pallas_call(functools.partial(window_kernel, modes, plan), out_shape=(...  40.8 us
    pallas_call x1, Pallas kernels, local(): pl.pallas_call(forward_kernel, in_specs=[SM] + [hbm] * 5, out_specs=VM, s...  4.13 us
    unnamed x16, local copies, waits for them, and re-layouts  2.39 us

profile of v4, /device:TPU:0, one launch (start us, length us, event | category | flops | bytes accessed | tf_op | source)
XLA Modules:
  0.0 50.4 jit_solution(9075873998828873423)
XLA Ops:
  0.6 0.0 copy-start.3
  0.6 0.0 copy-start
  0.7 0.0 copy-start.2
  0.7 0.0 copy-start.4
  0.7 0.0 copy-start.5
  0.7 0.0 copy-start.1
  3.0 4.1 %forward.1.row = f32[1,512]{1,0:T(1,128)} custom-call(s32[1]{0:T(128)S(6)} %copy.17.number, bf16[1,512,512]{2,1,0:T(8,128)(2,1)} %volume_hbm.1, bf16[2,512,512]{2,1,0:T(8,128)(2,1)} %constant.14.clone.fx_hbm, f32[4,5,16,512]{3,2,1,0:T(8,128)} %constant.15.clone.rot_hbm, bf16[2,4,512,512]{3,2,1,0:T(8,128)(2,1)} %constant.16.clone.mix_hbm, ...), custom_call_target="tpu_custom_call" | custom-call | tf_op jit(solution)/shard_map/forward/pallas_call | solution.py:505
  7.2 0.0 copy-done.3
  7.2 0.0 copy-done
  7.2 0.0 copy-done.2
  7.2 0.0 copy-done.4
  7.2 0.0 copy-done.5
  7.2 0.0 copy-done.1
  7.2 0.0 copy-start.6
  7.2 0.7 %copy-done.6 = f32[1,512]{1,0:T(1,128)S(1)} copy-done((f32[1,512]{1,0:T(1,128)S(1)}, f32[1,512]{1,0:T(1,128)}, u32[]{:S(2)}) %copy-start.6) | copy-done | bytes 2072
  7.9 40.8 %window.1 = (f32[1,128,512]{2,1,0:T(8,128)S(1)}, f32[256,8,128]{2,1,0:T(8,128)S(1)}) custom-call(s32[1,1]{1,0:T(1,128)S(6)} %copy.18.row_off, s32[1,1]{1,0:T(1,128)S(6)} %copy.19.col_off, s32[1]{0:T(128)S(6)} %copy.17.number, f32[1,512]{1,0:T(1,128)S(1)} %copy-done.6, f32[8,2,128,128]{3,2,1,0:T(8,128)S(1)} %copy-done.1, f32[1,1,128,128]{3,2,1,0:T(8,128)S(1)} %copy-done.5, ...), custom_call_target="tpu_custom_call" | custom-call | tf_op jit(solution)/shard_map/window/pallas_call | solution.py:529
  48.7 0.7 %copy.20 = f32[1,128,512]{2,1,0:T(8,128)} copy(f32[1,128,512]{2,1,0:T(8,128)S(1)} %get-tuple-element.8) | data formatting | bytes 524288
  49.4 1.0 %copy.21 = f32[8,2,128,128]{3,2,1,0:T(8,128)} copy(f32[8,2,128,128]{3,2,1,0:T(8,128)S(1)} %bitcast.1) | data formatting | bytes 2097152
Async XLA Ops:
  0.6 6.5 %copy-start.3 = (f32[5,16,512]{2,1,0:T(8,128)S(1)}, f32[5,16,512]{2,1,0:T(8,128)}, u32[]{:S(2)}) copy-start(f32[5,16,512]{2,1,0:T(8,128)} %constant.17.clone.wave_hbm) | copy-start | bytes 491524
  0.6 6.5 %copy-start = (f32[4,5,16,512]{3,2,1,0:T(8,128)S(1)}, f32[4,5,16,512]{3,2,1,0:T(8,128)}, u32[]{:S(2)}) copy-start(f32[4,5,16,512]{3,2,1,0:T(8,128)} %constant.15.clone.rot_hbm) | copy-start | bytes 1966084
  0.7 6.5 %copy-start.2 = (bf16[2,512,512]{2,1,0:T(8,128)(2,1)S(1)}, bf16[2,512,512]{2,1,0:T(8,128)(2,1)}, u32[]{:S(2)}) copy-start(bf16[2,512,512]{2,1,0:T(8,128)(2,1)} %constant.20.clone.fx_hbm) | copy-start | bytes 3145732
  0.7 6.5 %copy-start.4 = (bf16[2,2,256,256]{3,2,1,0:T(8,128)(2,1)S(1)}, bf16[2,2,256,256]{3,2,1,0:T(8,128)(2,1)}, u32[]{:S(2)}) copy-start(bf16[2,2,256,256]{3,2,1,0:T(8,128)(2,1)} %constant.18.clone.turn_hbm) | copy-start | bytes 1572868
  0.7 6.5 %copy-start.5 = (f32[1,1,128,128]{3,2,1,0:T(8,128)S(1)}, f32[1,1,128,128]{3,2,1,0:T(8,128)}, u32[]{:S(2)}) copy-start(f32[1,1,128,128]{3,2,1,0:T(8,128)} %measured_hbm.1) | copy-start | bytes 196612
  0.7 6.5 %copy-start.1 = (f32[8,2,128,128]{3,2,1,0:T(8,128)S(1)}, f32[8,2,128,128]{3,2,1,0:T(8,128)}, u32[]{:S(2)}) copy-start(f32[8,2,128,128]{3,2,1,0:T(8,128)} %probe_hbm.1) | copy-start | bytes 3145732
  7.2 0.7 %copy-start.6 = (f32[1,512]{1,0:T(1,128)S(1)}, f32[1,512]{1,0:T(1,128)}, u32[]{:S(2)}) copy-start(f32[1,512]{1,0:T(1,128)} %forward.1.row) | copy-start | bytes 6148

commit v5 on v4

--- a/solution.py
+++ b/solution.py
@@ -155,20 +155,15 @@
 
 
 def reduce_plan(angles, depth, tiles):
-    angle_bits = [("angle", 1 << b, 2) for b in range(angles.bit_length() - 1)]
     core = [("gz", 1, 2)]
+    along_xy = [("angle", 1, 4)] + [("angle", 1 << b, 2) for b in range(2, angles.bit_length() - 1)]
     along_z = [("gz", 2, 4)] + [("gz", 1 << b, 2) for b in range(3, depth.bit_length() - 1)]
-    along_x = core + angle_bits + along_z
-    along_y = core + angle_bits[::-1] + along_z
-    z_then_x = core + along_z + angle_bits
-    z_then_y = core + along_z + angle_bits[::-1]
+    xy_first = core + along_xy + along_z
+    z_first = core + along_z + along_xy
     unit = angles * depth
     if tiles != 8 * unit:
-        return [(along_x, tiles)]
-    return [
-        (along_x, 2 * unit), (along_y, 2 * unit), (z_then_x, unit),
-        (z_then_y, unit), (along_x, unit), (along_y, unit),
-    ]
+        return [(xy_first, tiles)]
+    return [(xy_first, 3 * unit), (z_first, unit), (xy_first, 3 * unit), (z_first, unit)]
 
 
 class Reducer:

time: 50.6 us -> 46 us (0.909)
  Pallas kernels: 44.9 us -> 40.3 us
    pallas_call x1, Pallas kernels: 40.8 us -> 36.2 us  [local(): pl.pallas_call(functools.partial(window_kernel, modes, plan), out_shape=(...]
where the time goes in v5:
time: 46 us; the launch traced here: 45.8 us
  Pallas kernels  40.3 us (88%)
  between operations  3.08 us (7%)
  local copies, waits for them, and re-layouts  2.39 us (5%)
    pallas_call x1, Pallas kernels, local(): pl.pallas_call(functools.partial(window_kernel, modes, plan), out_shape=(...  36.2 us
    pallas_call x1, Pallas kernels, local(): pl.pallas_call(forward_kernel, in_specs=[SM] + [hbm] * 5, out_specs=VM, s...  4.13 us
    unnamed x16, local copies, waits for them, and re-layouts  2.39 us

profile of v5, /device:TPU:0, one launch (start us, length us, event | category | flops | bytes accessed | tf_op | source)
XLA Modules:
  0.0 45.8 jit_solution(12901131851099810587)
XLA Ops:
  0.6 0.0 copy-start.3
  0.6 0.0 copy-start
  0.7 0.0 copy-start.2
  0.7 0.0 copy-start.4
  0.7 0.0 copy-start.5
  0.7 0.0 copy-start.1
  3.0 4.1 %forward.1.row = f32[1,512]{1,0:T(1,128)} custom-call(s32[1]{0:T(128)S(6)} %copy.17.number, bf16[1,512,512]{2,1,0:T(8,128)(2,1)} %volume_hbm.1, bf16[2,512,512]{2,1,0:T(8,128)(2,1)} %constant.14.clone.fx_hbm, f32[4,5,16,512]{3,2,1,0:T(8,128)} %constant.15.clone.rot_hbm, bf16[2,4,512,512]{3,2,1,0:T(8,128)(2,1)} %constant.16.clone.mix_hbm, ...), custom_call_target="tpu_custom_call" | custom-call | tf_op jit(solution)/shard_map/forward/pallas_call | solution.py:500
  7.2 0.0 copy-done.3
  7.2 0.0 copy-done
  7.2 0.0 copy-done.2
  7.2 0.0 copy-done.4
  7.2 0.0 copy-done.5
  7.2 0.0 copy-done.1
  7.2 0.0 copy-start.6
  7.2 0.7 %copy-done.6 = f32[1,512]{1,0:T(1,128)S(1)} copy-done((f32[1,512]{1,0:T(1,128)S(1)}, f32[1,512]{1,0:T(1,128)}, u32[]{:S(2)}) %copy-start.6) | copy-done | bytes 2072
  7.9 36.2 %window.1 = (f32[1,128,512]{2,1,0:T(8,128)S(1)}, f32[256,8,128]{2,1,0:T(8,128)S(1)}) custom-call(s32[1,1]{1,0:T(1,128)S(6)} %copy.18.row_off, s32[1,1]{1,0:T(1,128)S(6)} %copy.19.col_off, s32[1]{0:T(128)S(6)} %copy.17.number, f32[1,512]{1,0:T(1,128)S(1)} %copy-done.6, f32[8,2,128,128]{3,2,1,0:T(8,128)S(1)} %copy-done.1, f32[1,1,128,128]{3,2,1,0:T(8,128)S(1)} %copy-done.5, ...), custom_call_target="tpu_custom_call" | custom-call | tf_op jit(solution)/shard_map/window/pallas_call | solution.py:524
  44.1 0.7 %copy.20 = f32[1,128,512]{2,1,0:T(8,128)} copy(f32[1,128,512]{2,1,0:T(8,128)S(1)} %get-tuple-element.8) | data formatting | bytes 524288
  44.8 1.0 %copy.21 = f32[8,2,128,128]{3,2,1,0:T(8,128)} copy(f32[8,2,128,128]{3,2,1,0:T(8,128)S(1)} %bitcast.1) | data formatting | bytes 2097152
Async XLA Ops:
  0.6 6.5 %copy-start.3 = (f32[5,16,512]{2,1,0:T(8,128)S(1)}, f32[5,16,512]{2,1,0:T(8,128)}, u32[]{:S(2)}) copy-start(f32[5,16,512]{2,1,0:T(8,128)} %constant.17.clone.wave_hbm) | copy-start | bytes 491524
  0.6 6.5 %copy-start = (f32[4,5,16,512]{3,2,1,0:T(8,128)S(1)}, f32[4,5,16,512]{3,2,1,0:T(8,128)}, u32[]{:S(2)}) copy-start(f32[4,5,16,512]{3,2,1,0:T(8,128)} %constant.15.clone.rot_hbm) | copy-start | bytes 1966084
  0.7 6.5 %copy-start.2 = (bf16[2,512,512]{2,1,0:T(8,128)(2,1)S(1)}, bf16[2,512,512]{2,1,0:T(8,128)(2,1)}, u32[]{:S(2)}) copy-start(bf16[2,512,512]{2,1,0:T(8,128)(2,1)} %constant.20.clone.fx_hbm) | copy-start | bytes 3145732
  0.7 6.5 %copy-start.4 = (bf16[2,2,256,256]{3,2,1,0:T(8,128)(2,1)S(1)}, bf16[2,2,256,256]{3,2,1,0:T(8,128)(2,1)}, u32[]{:S(2)}) copy-start(bf16[2,2,256,256]{3,2,1,0:T(8,128)(2,1)} %constant.18.clone.turn_hbm) | copy-start | bytes 1572868
  0.7 6.5 %copy-start.5 = (f32[1,1,128,128]{3,2,1,0:T(8,128)S(1)}, f32[1,1,128,128]{3,2,1,0:T(8,128)}, u32[]{:S(2)}) copy-start(f32[1,1,128,128]{3,2,1,0:T(8,128)} %measured_hbm.1) | copy-start | bytes 196612
  0.7 6.5 %copy-start.1 = (f32[8,2,128,128]{3,2,1,0:T(8,128)S(1)}, f32[8,2,128,128]{3,2,1,0:T(8,128)}, u32[]{:S(2)}) copy-start(f32[8,2,128,128]{3,2,1,0:T(8,128)} %probe_hbm.1) | copy-start | bytes 3145732
  7.2 0.7 %copy-start.6 = (f32[1,512]{1,0:T(1,128)S(1)}, f32[1,512]{1,0:T(1,128)}, u32[]{:S(2)}) copy-start(f32[1,512]{1,0:T(1,128)} %forward.1.row) | copy-start | bytes 6148
